TPU v7x, 32 devices: a whole 2x2x4 slice. The times are simulated.
32 devices in a mesh: tm: 4 (over y, core), sx: 2 (over x), sy: 4 (over z).
Axes of the slice: x: 2, y: 2, z: 4, core: 2. Of those that a mesh axis runs over, the one named last changes fastest.
Arguments:
- state_old: float32 [4, 2, 128, 2048], P('tm', None, 'sx', 'sy'), may hold values from 0 to 1
- classes: int32 [128, 2048], P('sx', 'sy'), may hold values from 0 to 7
- seeds: int32 [128, 2048], P('sx', 'sy'), may hold values 0 or 1
- material_coef: float32 [4, 8], replicated, may hold values from 0.5 to 1
- coarse_decay: float32 [4, 2, 8], replicated, may hold values from 0 to 1, as said below
Outputs:
- new_states: float32 [4, 2, 128, 2048], P('tm', None, 'sx', 'sy')
Inputs may be any that keep to these rules, and one draw needn't show every extreme that they name: `coarse_decay`: each entry is a per-slice decay factor between 0 and 1.
All inputs are finite; a program needn't handle non-finite values. No bound on the sum of `seeds` on one device may be relied on, other than what follows from the above.
Results may differ from a plain program's by a relative error of at most 0.0001.
Values sent between devices are 32-bit elements; how exact they have to be, the bound alone decides.
A program may use at most 64 MiB of HBM per device.

v0:
```python
import jax
import jax.numpy as jnp
from jax import lax
from jax.sharding import PartitionSpec as P

SUBSTEPS = 4


def extended(cells, sides, width):
    for axis, dim in sides:
        count = lax.axis_size(axis)
        ends = count - 1
        head = lax.slice_in_dim(cells, 0, width, axis=dim)
        tail = lax.slice_in_dim(cells, cells.shape[dim] - width, cells.shape[dim], axis=dim)
        cells = jnp.concatenate(
            [
                lax.ppermute(tail, axis, [(i, (i + 1) % count) for i in range(ends)]),
                cells,
                lax.ppermute(head, axis, [((i + 1) % count, i) for i in range(ends)]),
            ],
            axis=dim,
        )
    return cells


def prefix(part, axis, combine, identity):
    place = lax.axis_index(axis)
    gathered = jax.tree.map(lambda a: lax.all_gather(a, axis), part)
    state = jax.tree.map(lambda a, e: jnp.zeros_like(a) + jnp.asarray(e, a.dtype), part, identity)

    def one(hop, state):
        return combine(
            state, jax.tree.map(lambda a: lax.dynamic_index_in_dim(a, hop, 0, False), gathered)
        )

    return lax.fori_loop(0, place, one, state)


def lookup(classes, coefficient_table):
    count = coefficient_table.shape[1]
    onehot = (classes[None, :, :] == jnp.arange(count, dtype=jnp.int32)[:, None, None]).astype(
        jnp.float32
    )
    return jnp.sum(coefficient_table[:, :, None, None] * onehot[None], axis=1)


def advance(padded, coef):
    centre = padded[:, 1:-1, 1:-1]
    lap = (
        padded[:, 2:, 1:-1]
        + padded[:, :-2, 1:-1]
        + padded[:, 1:-1, 2:]
        + padded[:, 1:-1, :-2]
        - 4.0 * centre
    )
    damage = centre[0]
    moist = centre[1]
    moist_new = moist + 0.24 * coef[0] * lap[1] - 0.05 * coef[3] * moist
    dryness = 1.0 - moist
    damage_new = (
        damage
        + 0.15 * coef[1] * lap[0]
        + 0.15 * (2.0 * (1.0 - damage) * coef[2] * dryness * dryness - damage)
    )
    damage_new = jnp.maximum(damage_new, coef[4])
    return jnp.stack([damage_new, moist_new])


def compose(earlier, later):
    return (later[0] * earlier[0], later[0] * earlier[1] + later[1])


def body(state_old, classes, seeds, material_coef, coarse_decay):
    start = state_old[0]
    coef = jnp.concatenate(
        [lookup(classes, material_coef), seeds.astype(jnp.float32)[None]], axis=0
    )
    state = start
    for step in range(SUBSTEPS):
        padded = extended(state, (("sx", 1), ("sy", 2)), 1)
        state = advance(padded, coef)
    slot = lax.axis_index("tm")
    table_now = lax.dynamic_index_in_dim(coarse_decay, slot, 0, keepdims=False)
    factor = lookup(classes, table_now)
    factor = jnp.where(slot == 0, jnp.float32(0.0), factor)
    offset = state - factor * start
    identity = (jnp.ones_like(factor), jnp.zeros_like(offset))
    before = prefix((factor, offset), "tm", compose, identity)
    result = factor * before[1] + offset
    return result[None]


def solution(mesh):
    return jax.shard_map(
        body,
        mesh=mesh,
        in_specs=(P("tm", None, "sx", "sy"), P("sx", "sy"), P("sx", "sy"), P(), P()),
        out_specs=P("tm", None, "sx", "sy"),
        check_vma=False,
    )
```

profile of v0, /device:TPU:13, one launch (start us, length us, event | category | flops | bytes accessed | tf_op | source)
XLA Modules:
  0.0 121.0 jit_solution(6295433291066933356)
XLA Ops:
  7.4 3.1 %collective-permute-start.1 = (f32[2,1,512]{2,1,0:T(1,128)S(1)}, f32[2,1,512]{2,1,0:T(1,128)S(1)}, u32[]{:S(2)}, u32[]{:S(2)}) collective-permute-start(f32[2,1,512]{2,1,0:T(1,128)S(1)} %get-tuple-element.78), channel_id=1, source_target_pairs={{0,4},{1,5},{2,6},{3,7},{8,12},{9,13},{10,14},{11,15},{16,20},{17,... | collective-permute-start | bytes 12296 | tf_op jit(solution)/shard_map/ppermute | solution.py:17
  12.8 2.0 %collective-permute-done = f32[2,1,512]{2,1,0:T(1,128)S(1)} collective-permute-done((f32[2,1,512]{2,1,0:T(1,128)S(1)}, f32[2,1,512]{2,1,0:T(1,128)S(1)}, u32[]{:S(2)}, u32[]{:S(2)}) %collective-permute-start) | collective-permute-done | bytes 4128 | tf_op jit(solution)/shard_map/ppermute | solution.py:19
  14.9 2.1 %collective-permute-start.2 = (f32[2,66,1]{2,1,0:T(8,128)S(1)}, f32[2,66,1]{2,1,0:T(8,128)S(1)}, u32[]{:S(2)}, u32[]{:S(2)}) collective-permute-start(f32[2,66,1]{2,1,0:T(8,128)S(1)} %get-tuple-element.70), channel_id=1, source_target_pairs={{1,0},{2,1},{3,2},{5,4},{6,5},{7,6},{9,8},{10,9},{11,10},{13,12},{... | collective-permute-start | bytes 1592 | tf_op jit(solution)/shard_map/ppermute | solution.py:19
  17.0 3.2 %collective-permute-start.3 = (f32[2,66,1]{2,1,0:T(8,128)S(1)}, f32[2,66,1]{2,1,0:T(8,128)S(1)}, u32[]{:S(2)}, u32[]{:S(2)}) collective-permute-start(f32[2,66,1]{2,1,0:T(8,128)S(1)} %get-tuple-element.71), channel_id=1, source_target_pairs={{0,1},{1,2},{2,3},{4,5},{5,6},{6,7},{8,9},{9,10},{10,11},{12,13},{... | collective-permute-start | bytes 1592 | tf_op jit(solution)/shard_map/ppermute | solution.py:17
  20.6 1.8 %collective-permute-done.3 = f32[2,66,1]{2,1,0:T(8,128)S(1)} collective-permute-done((f32[2,66,1]{2,1,0:T(8,128)S(1)}, f32[2,66,1]{2,1,0:T(8,128)S(1)}, u32[]{:S(2)}, u32[]{:S(2)}) %collective-permute-start.3) | collective-permute-done | bytes 560 | tf_op jit(solution)/shard_map/ppermute | solution.py:17
  22.8 1.8 %collective-permute-start.5 = (f32[2,1,512]{2,1,0:T(1,128)S(1)}, f32[2,1,512]{2,1,0:T(1,128)S(1)}, u32[]{:S(2)}, u32[]{:S(2)}) collective-permute-start(f32[2,1,512]{2,1,0:T(1,128)S(1)} %get-tuple-element.76), channel_id=1, source_target_pairs={{0,4},{1,5},{2,6},{3,7},{8,12},{9,13},{10,14},{11,15},{16,20},{17,... | collective-permute-start | bytes 12296 | tf_op jit(solution)/shard_map/ppermute | solution.py:17
  24.7 1.3 %collective-permute-start.4 = (f32[2,1,512]{2,1,0:T(1,128)S(1)}, f32[2,1,512]{2,1,0:T(1,128)S(1)}, u32[]{:S(2)}, u32[]{:S(2)}) collective-permute-start(f32[2,1,512]{2,1,0:T(1,128)S(1)} %get-tuple-element.77), channel_id=1, source_target_pairs={{4,0},{5,1},{6,2},{7,3},{12,8},{13,9},{14,10},{15,11},{20,16},{21,... | collective-permute-start | bytes 12296 | tf_op jit(solution)/shard_map/ppermute | solution.py:19
  26.0 3.0 %collective-permute-done.4 = f32[2,1,512]{2,1,0:T(1,128)S(1)} collective-permute-done((f32[2,1,512]{2,1,0:T(1,128)S(1)}, f32[2,1,512]{2,1,0:T(1,128)S(1)}, u32[]{:S(2)}, u32[]{:S(2)}) %collective-permute-start.4) | collective-permute-done | bytes 4128 | tf_op jit(solution)/shard_map/ppermute | solution.py:19
  29.1 1.9 %collective-permute-start.6 = (f32[2,66,1]{2,1,0:T(8,128)S(1)}, f32[2,66,1]{2,1,0:T(8,128)S(1)}, u32[]{:S(2)}, u32[]{:S(2)}) collective-permute-start(f32[2,66,1]{2,1,0:T(8,128)S(1)} %get-tuple-element.68), channel_id=1, source_target_pairs={{1,0},{2,1},{3,2},{5,4},{6,5},{7,6},{9,8},{10,9},{11,10},{13,12},{... | collective-permute-start | bytes 1592 | tf_op jit(solution)/shard_map/ppermute | solution.py:19
  31.1 3.4 %collective-permute-start.7 = (f32[2,66,1]{2,1,0:T(8,128)S(1)}, f32[2,66,1]{2,1,0:T(8,128)S(1)}, u32[]{:S(2)}, u32[]{:S(2)}) collective-permute-start(f32[2,66,1]{2,1,0:T(8,128)S(1)} %get-tuple-element.69), channel_id=1, source_target_pairs={{0,1},{1,2},{2,3},{4,5},{5,6},{6,7},{8,9},{9,10},{10,11},{12,13},{... | collective-permute-start | bytes 1592 | tf_op jit(solution)/shard_map/ppermute | solution.py:17
  34.5 1.7 %collective-permute-done.7 = f32[2,66,1]{2,1,0:T(8,128)S(1)} collective-permute-done((f32[2,66,1]{2,1,0:T(8,128)S(1)}, f32[2,66,1]{2,1,0:T(8,128)S(1)}, u32[]{:S(2)}, u32[]{:S(2)}) %collective-permute-start.7) | collective-permute-done | bytes 560 | tf_op jit(solution)/shard_map/ppermute | solution.py:17
  36.6 1.7 %collective-permute-start.9 = (f32[2,1,512]{2,1,0:T(1,128)S(1)}, f32[2,1,512]{2,1,0:T(1,128)S(1)}, u32[]{:S(2)}, u32[]{:S(2)}) collective-permute-start(f32[2,1,512]{2,1,0:T(1,128)S(1)} %get-tuple-element.74), channel_id=1, source_target_pairs={{0,4},{1,5},{2,6},{3,7},{8,12},{9,13},{10,14},{11,15},{16,20},{17,... | collective-permute-start | bytes 12296 | tf_op jit(solution)/shard_map/ppermute | solution.py:17
  39.6 3.0 %collective-permute-done.8 = f32[2,1,512]{2,1,0:T(1,128)S(1)} collective-permute-done((f32[2,1,512]{2,1,0:T(1,128)S(1)}, f32[2,1,512]{2,1,0:T(1,128)S(1)}, u32[]{:S(2)}, u32[]{:S(2)}) %collective-permute-start.8) | collective-permute-done | bytes 4128 | tf_op jit(solution)/shard_map/ppermute | solution.py:19
  42.7 1.9 %collective-permute-start.10 = (f32[2,66,1]{2,1,0:T(8,128)S(1)}, f32[2,66,1]{2,1,0:T(8,128)S(1)}, u32[]{:S(2)}, u32[]{:S(2)}) collective-permute-start(f32[2,66,1]{2,1,0:T(8,128)S(1)} %get-tuple-element.66), channel_id=1, source_target_pairs={{1,0},{2,1},{3,2},{5,4},{6,5},{7,6},{9,8},{10,9},{11,10},{13,12},{... | collective-permute-start | bytes 1592 | tf_op jit(solution)/shard_map/ppermute | solution.py:19
  44.7 3.4 %collective-permute-start.11 = (f32[2,66,1]{2,1,0:T(8,128)S(1)}, f32[2,66,1]{2,1,0:T(8,128)S(1)}, u32[]{:S(2)}, u32[]{:S(2)}) collective-permute-start(f32[2,66,1]{2,1,0:T(8,128)S(1)} %get-tuple-element.67), channel_id=1, source_target_pairs={{0,1},{1,2},{2,3},{4,5},{5,6},{6,7},{8,9},{9,10},{10,11},{12,13},{... | collective-permute-start | bytes 1592 | tf_op jit(solution)/shard_map/ppermute | solution.py:17
  48.1 1.7 %collective-permute-done.11 = f32[2,66,1]{2,1,0:T(8,128)S(1)} collective-permute-done((f32[2,66,1]{2,1,0:T(8,128)S(1)}, f32[2,66,1]{2,1,0:T(8,128)S(1)}, u32[]{:S(2)}, u32[]{:S(2)}) %collective-permute-start.11) | collective-permute-done | bytes 560 | tf_op jit(solution)/shard_map/ppermute | solution.py:17
  50.2 1.7 %collective-permute-start.13 = (f32[2,1,512]{2,1,0:T(1,128)S(1)}, f32[2,1,512]{2,1,0:T(1,128)S(1)}, u32[]{:S(2)}, u32[]{:S(2)}) collective-permute-start(f32[2,1,512]{2,1,0:T(1,128)S(1)} %get-tuple-element.72), channel_id=1, source_target_pairs={{0,4},{1,5},{2,6},{3,7},{8,12},{9,13},{10,14},{11,15},{16,20},{17,... | collective-permute-start | bytes 12296 | tf_op jit(solution)/shard_map/ppermute | solution.py:17
  53.2 3.3 %collective-permute-done.12 = f32[2,1,512]{2,1,0:T(1,128)S(1)} collective-permute-done((f32[2,1,512]{2,1,0:T(1,128)S(1)}, f32[2,1,512]{2,1,0:T(1,128)S(1)}, u32[]{:S(2)}, u32[]{:S(2)}) %collective-permute-start.12) | collective-permute-done | bytes 4128 | tf_op jit(solution)/shard_map/ppermute | solution.py:19
  56.6 1.9 %collective-permute-start.14 = (f32[2,66,1]{2,1,0:T(8,128)S(1)}, f32[2,66,1]{2,1,0:T(8,128)S(1)}, u32[]{:S(2)}, u32[]{:S(2)}) collective-permute-start(f32[2,66,1]{2,1,0:T(8,128)S(1)} %get-tuple-element.64), channel_id=1, source_target_pairs={{1,0},{2,1},{3,2},{5,4},{6,5},{7,6},{9,8},{10,9},{11,10},{13,12},{... | collective-permute-start | bytes 1592 | tf_op jit(solution)/shard_map/ppermute | solution.py:19
  58.6 3.4 %collective-permute-start.15 = (f32[2,66,1]{2,1,0:T(8,128)S(1)}, f32[2,66,1]{2,1,0:T(8,128)S(1)}, u32[]{:S(2)}, u32[]{:S(2)}) collective-permute-start(f32[2,66,1]{2,1,0:T(8,128)S(1)} %get-tuple-element.65), channel_id=1, source_target_pairs={{0,1},{1,2},{2,3},{4,5},{5,6},{6,7},{8,9},{9,10},{10,11},{12,13},{... | collective-permute-start | bytes 1592 | tf_op jit(solution)/shard_map/ppermute | solution.py:17
  62.2 1.5 %collective-permute-done.15 = f32[2,66,1]{2,1,0:T(8,128)S(1)} collective-permute-done((f32[2,66,1]{2,1,0:T(8,128)S(1)}, f32[2,66,1]{2,1,0:T(8,128)S(1)}, u32[]{:S(2)}, u32[]{:S(2)}) %collective-permute-start.15) | collective-permute-done | bytes 560 | tf_op jit(solution)/shard_map/ppermute | solution.py:17
  65.7 25.6 %all-gather.4.cloned.1.call-done = f32[4,2,64,512]{3,2,1,0:T(8,128)} async-done(((f32[1,2,64,512]{3,2,1,0:T(8,128)}), f32[4,2,64,512]{3,2,1,0:T(8,128)}) %all-gather.4.cloned.1.call-update) | async-done | bytes 1048592 | tf_op jit(solution)/shard_map/all_gather | solution.py:28
  91.3 18.3 %all-gather.6.cloned.1.call-done = f32[8,64,512]{2,1,0:T(8,128)} async-done(((f32[2,64,512]{2,1,0:T(8,128)}), f32[8,64,512]{2,1,0:T(8,128)}) %all-gather.6.cloned.1.call-update) | async-done | bytes 1048592 | tf_op jit(solution)/shard_map/all_gather | solution.py:28
  109.7 3.6 %while.12 = (s32[]{:T(128)}, f32[2,64,512]{2,1,0:T(8,128)S(1)}, s32[]{:T(128)}, f32[4,2,64,512]{3,2,1,0:T(8,128)}, f32[4,2,64,512]{3,2,1,0:T(8,128)}, /*index=5*/s32[]{:T(128)}, s32[]{:T(128)}, s32[]{:T(128)}) while((s32[]{:T(128)}, f32[2,64,512]{2,1,0:T(8,128)S(1)}, s32[]{:T(128)}, f32[4,2,64,512]{3,2,1,0:T(8,128)}, ...), condition=%wide.region_3.4_spmd, body=%wide.region_2.3_spmd.sunk | while | flops 131077 | bytes 1048707 | solution.py:36
  (55 shorter events, 14.4 us)
Async XLA Ops:
  6.5 46.7 %copy-start = (f32[4,2,8]{2,1,0:T(2,128)S(1)}, f32[4,2,8]{2,1,0:T(2,128)}, u32[]{:S(2)}) copy-start(f32[4,2,8]{2,1,0:T(2,128)} %param.11) | copy-start | bytes 772
  6.5 8.3 %copy-start.1 = (f32[1,2,64,512]{3,2,1,0:T(8,128)S(1)}, f32[1,2,64,512]{3,2,1,0:T(8,128)}, u32[]{:S(2)}) copy-start(f32[1,2,64,512]{3,2,1,0:T(8,128)} %param.7) | copy-start | bytes 786436
  6.5 13.7 %copy-start.4 = (f32[4,8]{1,0:T(4,128)S(1)}, f32[4,8]{1,0:T(4,128)}, u32[]{:S(2)}) copy-start(f32[4,8]{1,0:T(4,128)} %param.10) | copy-start | bytes 388
  6.5 84.8 %all-gather.4.cloned.1.call-start = ((), (), s32[]{:S(2)}) async-start(), calls=%async_computation | async-start | bytes 1310720 | tf_op jit(solution)/shard_map/all_gather | solution.py:28
  7.4 5.5 %collective-permute-start.1 = (f32[2,1,512]{2,1,0:T(1,128)S(1)}, f32[2,1,512]{2,1,0:T(1,128)S(1)}, u32[]{:S(2)}, u32[]{:S(2)}) collective-permute-start(f32[2,1,512]{2,1,0:T(1,128)S(1)} %get-tuple-element.78), channel_id=1, source_target_pairs={{0,4},{1,5},{2,6},{3,7},{8,12},{9,13},{10,14},{11,15},{16,20},{17,... | collective-permute-start | bytes 12296 | tf_op jit(solution)/shard_map/ppermute | solution.py:17
  10.5 4.4 %collective-permute-start = (f32[2,1,512]{2,1,0:T(1,128)S(1)}, f32[2,1,512]{2,1,0:T(1,128)S(1)}, u32[]{:S(2)}, u32[]{:S(2)}) collective-permute-start(f32[2,1,512]{2,1,0:T(1,128)S(1)} %get-tuple-element.79), channel_id=1, source_target_pairs={{4,0},{5,1},{6,2},{7,3},{12,8},{13,9},{14,10},{15,11},{20,16},{21,... | collective-permute-start | bytes 12296 | tf_op jit(solution)/shard_map/ppermute | solution.py:19
  14.9 5.7 %collective-permute-start.2 = (f32[2,66,1]{2,1,0:T(8,128)S(1)}, f32[2,66,1]{2,1,0:T(8,128)S(1)}, u32[]{:S(2)}, u32[]{:S(2)}) collective-permute-start(f32[2,66,1]{2,1,0:T(8,128)S(1)} %get-tuple-element.70), channel_id=1, source_target_pairs={{1,0},{2,1},{3,2},{5,4},{6,5},{7,6},{9,8},{10,9},{11,10},{13,12},{... | collective-permute-start | bytes 1592 | tf_op jit(solution)/shard_map/ppermute | solution.py:19
  17.0 5.4 %collective-permute-start.3 = (f32[2,66,1]{2,1,0:T(8,128)S(1)}, f32[2,66,1]{2,1,0:T(8,128)S(1)}, u32[]{:S(2)}, u32[]{:S(2)}) collective-permute-start(f32[2,66,1]{2,1,0:T(8,128)S(1)} %get-tuple-element.71), channel_id=1, source_target_pairs={{0,1},{1,2},{2,3},{4,5},{5,6},{6,7},{8,9},{9,10},{10,11},{12,13},{... | collective-permute-start | bytes 1592 | tf_op jit(solution)/shard_map/ppermute | solution.py:17
  20.6 2.1 %copy-start.3 = (s32[64,512]{1,0:T(8,128)S(1)}, s32[64,512]{1,0:T(8,128)}, u32[]{:S(2)}) copy-start(s32[64,512]{1,0:T(8,128)} %param.9) | copy-start | bytes 393220
  22.8 3.2 %collective-permute-start.5 = (f32[2,1,512]{2,1,0:T(1,128)S(1)}, f32[2,1,512]{2,1,0:T(1,128)S(1)}, u32[]{:S(2)}, u32[]{:S(2)}) collective-permute-start(f32[2,1,512]{2,1,0:T(1,128)S(1)} %get-tuple-element.76), channel_id=1, source_target_pairs={{0,4},{1,5},{2,6},{3,7},{8,12},{9,13},{10,14},{11,15},{16,20},{17,... | collective-permute-start | bytes 12296 | tf_op jit(solution)/shard_map/ppermute | solution.py:17
  24.7 4.4 %collective-permute-start.4 = (f32[2,1,512]{2,1,0:T(1,128)S(1)}, f32[2,1,512]{2,1,0:T(1,128)S(1)}, u32[]{:S(2)}, u32[]{:S(2)}) collective-permute-start(f32[2,1,512]{2,1,0:T(1,128)S(1)} %get-tuple-element.77), channel_id=1, source_target_pairs={{4,0},{5,1},{6,2},{7,3},{12,8},{13,9},{14,10},{15,11},{20,16},{21,... | collective-permute-start | bytes 12296 | tf_op jit(solution)/shard_map/ppermute | solution.py:19
  29.1 5.3 %collective-permute-start.6 = (f32[2,66,1]{2,1,0:T(8,128)S(1)}, f32[2,66,1]{2,1,0:T(8,128)S(1)}, u32[]{:S(2)}, u32[]{:S(2)}) collective-permute-start(f32[2,66,1]{2,1,0:T(8,128)S(1)} %get-tuple-element.68), channel_id=1, source_target_pairs={{1,0},{2,1},{3,2},{5,4},{6,5},{7,6},{9,8},{10,9},{11,10},{13,12},{... | collective-permute-start | bytes 1592 | tf_op jit(solution)/shard_map/ppermute | solution.py:19
  31.1 5.1 %collective-permute-start.7 = (f32[2,66,1]{2,1,0:T(8,128)S(1)}, f32[2,66,1]{2,1,0:T(8,128)S(1)}, u32[]{:S(2)}, u32[]{:S(2)}) collective-permute-start(f32[2,66,1]{2,1,0:T(8,128)S(1)} %get-tuple-element.69), channel_id=1, source_target_pairs={{0,1},{1,2},{2,3},{4,5},{5,6},{6,7},{8,9},{9,10},{10,11},{12,13},{... | collective-permute-start | bytes 1592 | tf_op jit(solution)/shard_map/ppermute | solution.py:17
  36.6 3.0 %collective-permute-start.9 = (f32[2,1,512]{2,1,0:T(1,128)S(1)}, f32[2,1,512]{2,1,0:T(1,128)S(1)}, u32[]{:S(2)}, u32[]{:S(2)}) collective-permute-start(f32[2,1,512]{2,1,0:T(1,128)S(1)} %get-tuple-element.74), channel_id=1, source_target_pairs={{0,4},{1,5},{2,6},{3,7},{8,12},{9,13},{10,14},{11,15},{16,20},{17,... | collective-permute-start | bytes 12296 | tf_op jit(solution)/shard_map/ppermute | solution.py:17
  38.3 4.4 %collective-permute-start.8 = (f32[2,1,512]{2,1,0:T(1,128)S(1)}, f32[2,1,512]{2,1,0:T(1,128)S(1)}, u32[]{:S(2)}, u32[]{:S(2)}) collective-permute-start(f32[2,1,512]{2,1,0:T(1,128)S(1)} %get-tuple-element.75), channel_id=1, source_target_pairs={{4,0},{5,1},{6,2},{7,3},{12,8},{13,9},{14,10},{15,11},{20,16},{21,... | collective-permute-start | bytes 12296 | tf_op jit(solution)/shard_map/ppermute | solution.py:19
  42.7 5.3 %collective-permute-start.10 = (f32[2,66,1]{2,1,0:T(8,128)S(1)}, f32[2,66,1]{2,1,0:T(8,128)S(1)}, u32[]{:S(2)}, u32[]{:S(2)}) collective-permute-start(f32[2,66,1]{2,1,0:T(8,128)S(1)} %get-tuple-element.66), channel_id=1, source_target_pairs={{1,0},{2,1},{3,2},{5,4},{6,5},{7,6},{9,8},{10,9},{11,10},{13,12},{... | collective-permute-start | bytes 1592 | tf_op jit(solution)/shard_map/ppermute | solution.py:19
  44.7 5.1 %collective-permute-start.11 = (f32[2,66,1]{2,1,0:T(8,128)S(1)}, f32[2,66,1]{2,1,0:T(8,128)S(1)}, u32[]{:S(2)}, u32[]{:S(2)}) collective-permute-start(f32[2,66,1]{2,1,0:T(8,128)S(1)} %get-tuple-element.67), channel_id=1, source_target_pairs={{0,1},{1,2},{2,3},{4,5},{5,6},{6,7},{8,9},{9,10},{10,11},{12,13},{... | collective-permute-start | bytes 1592 | tf_op jit(solution)/shard_map/ppermute | solution.py:17
  50.2 3.0 %collective-permute-start.13 = (f32[2,1,512]{2,1,0:T(1,128)S(1)}, f32[2,1,512]{2,1,0:T(1,128)S(1)}, u32[]{:S(2)}, u32[]{:S(2)}) collective-permute-start(f32[2,1,512]{2,1,0:T(1,128)S(1)} %get-tuple-element.72), channel_id=1, source_target_pairs={{0,4},{1,5},{2,6},{3,7},{8,12},{9,13},{10,14},{11,15},{16,20},{17,... | collective-permute-start | bytes 12296 | tf_op jit(solution)/shard_map/ppermute | solution.py:17
  51.9 4.6 %collective-permute-start.12 = (f32[2,1,512]{2,1,0:T(1,128)S(1)}, f32[2,1,512]{2,1,0:T(1,128)S(1)}, u32[]{:S(2)}, u32[]{:S(2)}) collective-permute-start(f32[2,1,512]{2,1,0:T(1,128)S(1)} %get-tuple-element.73), channel_id=1, source_target_pairs={{4,0},{5,1},{6,2},{7,3},{12,8},{13,9},{14,10},{15,11},{20,16},{21,... | collective-permute-start | bytes 12296 | tf_op jit(solution)/shard_map/ppermute | solution.py:19
  56.6 5.5 %collective-permute-start.14 = (f32[2,66,1]{2,1,0:T(8,128)S(1)}, f32[2,66,1]{2,1,0:T(8,128)S(1)}, u32[]{:S(2)}, u32[]{:S(2)}) collective-permute-start(f32[2,66,1]{2,1,0:T(8,128)S(1)} %get-tuple-element.64), channel_id=1, source_target_pairs={{1,0},{2,1},{3,2},{5,4},{6,5},{7,6},{9,8},{10,9},{11,10},{13,12},{... | collective-permute-start | bytes 1592 | tf_op jit(solution)/shard_map/ppermute | solution.py:19
  58.6 5.1 %collective-permute-start.15 = (f32[2,66,1]{2,1,0:T(8,128)S(1)}, f32[2,66,1]{2,1,0:T(8,128)S(1)}, u32[]{:S(2)}, u32[]{:S(2)}) collective-permute-start(f32[2,66,1]{2,1,0:T(8,128)S(1)} %get-tuple-element.65), channel_id=1, source_target_pairs={{0,1},{1,2},{2,3},{4,5},{5,6},{6,7},{8,9},{9,10},{10,11},{12,13},{... | collective-permute-start | bytes 1592 | tf_op jit(solution)/shard_map/ppermute | solution.py:17
  65.0 44.7 %all-gather.6.cloned.1.call-start = ((), (), s32[]{:S(2)}) async-start(), calls=%async_computation.1 | async-start | bytes 1310720 | tf_op jit(solution)/shard_map/all_gather | solution.py:28
  109.7 3.6 %copy-start.2 = (f32[2,64,512]{2,1,0:T(8,128)S(1)}, f32[2,64,512]{2,1,0:T(8,128)}, u32[]{:S(2)}) copy-start(f32[2,64,512]{2,1,0:T(8,128)} %get-tuple-element.61) | copy-start | bytes 786436
Sparse Core Ops, SparseCore 0:
  65.1 26.1 all-gather.3
  92.9 16.7 all-gather.5
where the time goes:
time: 122 us; the launch traced here: 121 us
  waiting for transfers between devices  62.7 us (51%)
  starting transfers between devices  34.6 us (28%)
  between operations  13.8 us (11%)
  other arithmetic  8.83 us (7%)
    all_gather x2, waiting for transfers between devices, prefix(): gathered = jax.tree.map(lambda a: lax.all_gather(a, axis), part)  43.9 us
    ppermute x8, starting transfers between devices, extended(): lax.ppermute(tail, axis, [(i, (i + 1) % count) for i in range(ends)])  21.6 us
    ppermute x8, starting transfers between devices, extended(): lax.ppermute(head, axis, [((i + 1) % count, i) for i in range(ends)])  13 us
    ppermute x8, waiting for transfers between devices, extended(): lax.ppermute(head, axis, [((i + 1) % count, i) for i in range(ends)])  11.4 us
    ppermute x8, waiting for transfers between devices, extended(): lax.ppermute(tail, axis, [(i, (i + 1) % count) for i in range(ends)])  6.71 us
    add x3, other arithmetic, compose(): return (later[0] * earlier[0], later[0] * earlier[1] + later[1])  3.56 us
  transfers between devices with their start and end apart: 18, of which 10 were waited for; matrix products, arithmetic and copies ran while one was open for 1% of the time, Pallas kernels for 0%

commit v1 on v0

v1 whole, which is shorter than its diff:
```python
import functools

import jax
import jax.numpy as jnp
from jax import lax
from jax.experimental import pallas as pl
from jax.experimental.pallas import tpu as pltpu
from jax.sharding import PartitionSpec as P

SUBSTEPS = 4
LANES = 128
ROWS = 8
TABLES = 5


def pick(bits, values):
    for bit in bits:
        values = [jnp.where(bit, values[2 * i + 1], values[2 * i]) for i in range(len(values) // 2)]
    return values[0]


def bits_of(classes):
    return [(classes & (1 << b)) != 0 for b in range(3)]


def kernel(
    sizes, state_hbm, classes_hbm, seeds_hbm, mat, decay, out_hbm,
    start, ping, pong, coef, factor, cls, sds, inbox, outbox,
    row_out, row_in, col_out, col_in, diag_in,
    load_sem, row_send, row_recv, col_send, col_recv, diag_send, diag_recv, chain_send, chain_recv, store_sem,
):
    n_t, n_x, n_y, height, width = sizes
    groups = height // ROWS
    slot, px, py = lax.axis_index("tm"), lax.axis_index("sx"), lax.axis_index("sy")
    f32 = jnp.float32

    has_x = [px > 0, px < n_x - 1]
    has_y = [py > 0, py < n_y - 1]
    to_x = [px - 1, px + 1]
    to_y = [py - 1, py + 1]
    peers = []
    for a in range(2):
        peers.append((has_x[a], {"sx": to_x[a]}))
        peers.append((has_y[a], {"sy": to_y[a]}))
        for b in range(2):
            peers.append((jnp.logical_and(has_x[a], has_y[b]), {"sx": to_x[a], "sy": to_y[b]}))
    peers.append((slot > 0, {"tm": slot - 1}))
    peers.append((slot < n_t - 1, {"tm": slot + 1}))

    loads = [
        pltpu.make_async_copy(state_hbm, start.at[:, pl.ds(0, height), pl.ds(0, width)], load_sem.at[0]),
        pltpu.make_async_copy(classes_hbm, cls, load_sem.at[1]),
        pltpu.make_async_copy(seeds_hbm, sds, load_sem.at[2]),
    ]
    for load in loads:
        load.start()

    barrier = pltpu.get_barrier_semaphore()
    total = jnp.int32(0)
    for there, where in peers:
        total = total + there.astype(jnp.int32)

        @pl.when(there)
        def _():
            pl.semaphore_signal(barrier, inc=1, device_id=where, device_id_type=pl.DeviceIdType.MESH)

    for load in loads:
        load.wait()

    lane = lax.broadcasted_iota(jnp.int32, (ROWS, LANES), 1)
    sub = lax.broadcasted_iota(jnp.int32, (ROWS, LANES), 0)
    sub_wide = lax.broadcasted_iota(jnp.int32, (ROWS, width), 0)

    def field(f, rows, cols):
        if f < 2:
            return start[f, rows, cols]
        return (cls if f == 2 else sds)[rows, cols].astype(f32)

    for side in range(2):
        rows = pl.ds(0, ROWS) if side == 0 else pl.ds(height - ROWS, ROWS)
        keep = (sub_wide < 4) if side == 0 else (sub_wide >= 4)
        for pair in range(2):
            one = field(2 * pair, rows, pl.ds(0, width))
            two = pltpu.roll(field(2 * pair + 1, rows, pl.ds(0, width)), 4, 0)
            row_out[side, pl.ds(ROWS * pair, ROWS), :] = jnp.where(keep, one, two)
    for side in range(2):
        cols = pl.ds(0, LANES) if side == 0 else pl.ds(width - LANES, LANES)
        packed = jnp.zeros((ROWS, LANES), f32)
        for g in range(groups):
            for f in range(4):
                at = 16 * g + 4 * f
                tile = field(f, pl.ds(ROWS * g, ROWS), cols)
                shift = (at if side == 0 else at + 4) % LANES
                if shift:
                    tile = pltpu.roll(tile, shift, 1)
                packed = jnp.where((lane >= at) & (lane < at + 4), tile, packed)
        col_out[side] = packed

    pl.semaphore_wait(barrier, total)

    sends = []
    for a in range(2):
        sends.append((has_x[a], has_x[1 - a], pltpu.make_async_remote_copy(
            row_out.at[a], row_in.at[1 - a], row_send.at[a], row_recv.at[1 - a],
            device_id={"sx": to_x[a]}, device_id_type=pl.DeviceIdType.MESH)))
        sends.append((has_y[a], has_y[1 - a], pltpu.make_async_remote_copy(
            col_out.at[a], col_in.at[1 - a], col_send.at[a], col_recv.at[1 - a],
            device_id={"sy": to_y[a]}, device_id_type=pl.DeviceIdType.MESH)))
        for b in range(2):
            sends.append((
                jnp.logical_and(has_x[a], has_y[b]), jnp.logical_and(has_x[1 - a], has_y[1 - b]),
                pltpu.make_async_remote_copy(
                    col_out.at[b], diag_in.at[1 - a, 1 - b], diag_send.at[a, b], diag_recv.at[1 - a, 1 - b],
                    device_id={"sx": to_x[a], "sy": to_y[b]}, device_id_type=pl.DeviceIdType.MESH)))
    for there, _, copy in sends:
        @pl.when(there)
        def _():
            copy.start()

    for a in range(2):
        @pl.when(jnp.logical_not(has_x[a]))
        def _():
            row_in[a] = jnp.zeros_like(row_in[a])

        @pl.when(jnp.logical_not(has_y[a]))
        def _():
            col_in[a] = jnp.zeros_like(col_in[a])

        for b in range(2):
            @pl.when(jnp.logical_not(jnp.logical_and(has_x[a], has_y[b])))
            def _():
                diag_in[a, b] = jnp.zeros_like(diag_in[a, b])

    c0, c1, c2, c3 = [[mat[i, c] for c in range(8)] for i in range(4)]
    tables = [
        [0.24 * c0[c] for c in range(8)],
        [1.0 - 0.96 * c0[c] - 0.05 * c3[c] for c in range(8)],
        [0.15 * c1[c] for c in range(8)],
        [0.85 - 0.6 * c1[c] for c in range(8)],
        [0.3 * c2[c] for c in range(8)],
    ]
    factors = [[decay[slot, f, c] for c in range(8)] for f in range(2)]

    for g in range(groups):
        rows = pl.ds(ROWS * g, ROWS)
        bits = bits_of(cls[rows, :])
        for t in range(TABLES):
            coef[t, rows, pl.ds(0, width)] = pick(bits, tables[t])
        coef[TABLES, rows, pl.ds(0, width)] = sds[rows, :].astype(f32)
        for f in range(2):
            factor[f, rows, :] = pick(bits, factors[f])

    for _, here, copy in sends:
        @pl.when(here)
        def _():
            copy.wait_recv()

    def fill(rows, cols, values, mask):
        start[0, rows, cols] = values[0]
        start[1, rows, cols] = values[1]
        bits = bits_of(values[2].astype(jnp.int32))
        for t in range(TABLES):
            coef[t, rows, cols] = pick(bits, tables[t]) * mask
        coef[TABLES, rows, cols] = values[3] * mask

    as_f = lambda flag: flag.astype(jnp.int32).astype(f32)
    flag_x = [as_f(v) for v in has_x]
    flag_y = [as_f(v) for v in has_y]

    low = sub_wide < 4
    values = []
    for pair in range(2):
        below = row_in[1, pl.ds(ROWS * pair, ROWS), :]
        above = row_in[0, pl.ds(ROWS * pair, ROWS), :]
        values.append(jnp.where(low, below, above))
        values.append(pltpu.roll(jnp.where(low, above, below), 4, 0))
    fill(pl.ds(height, ROWS), pl.ds(0, width), values, jnp.where(low, flag_x[1], flag_x[0]))

    first, last = lane < 4, lane >= LANES - 4
    col_mask = jnp.where(first, flag_y[1], jnp.where(last, flag_y[0], 0.0))

    def unpack(right, left, g, f):
        at = 16 * g + 4 * f
        r = pltpu.roll(right, (LANES - at) % LANES, 1) if at else right
        l = pltpu.roll(left, (LANES - 4 - at) % LANES, 1) if at != LANES - 4 else left
        return jnp.where(first, r, jnp.where(last, l, 0.0))

    right, left = col_in[1], col_in[0]
    for g in range(groups):
        fill(
            pl.ds(ROWS * g, ROWS), pl.ds(width, LANES),
            [unpack(right, left, g, f) for f in range(4)], col_mask,
        )
    low = sub < 4
    values = []
    for f in range(4):
        below = unpack(diag_in[1, 1], diag_in[1, 0], 0, f)
        above = unpack(diag_in[0, 1], diag_in[0, 0], groups - 1, f)
        values.append(jnp.where(low, below, above))
    fill(
        pl.ds(height, ROWS), pl.ds(width, LANES), values,
        col_mask * jnp.where(low, flag_x[1], flag_x[0]),
    )

    full = width + LANES
    sub_full = lax.broadcasted_iota(jnp.int32, (ROWS, full), 0)
    count = groups + 1

    def around(x, before, after):
        up = jnp.where(sub_full == 0, pltpu.roll(before, 1, 0), pltpu.roll(x, 1, 0))
        down = jnp.where(sub_full == ROWS - 1, pltpu.roll(after, ROWS - 1, 0), pltpu.roll(x, ROWS - 1, 0))
        return up + down + pltpu.roll(x, 1, 1) + pltpu.roll(x, full - 1, 1)

    def advance(src, g):
        rows = pl.ds(ROWS * g, ROWS)
        near = [pl.ds(ROWS * ((g - 1) % count), ROWS), pl.ds(ROWS * ((g + 1) % count), ROWS)]
        d, m = src[0, rows, :], src[1, rows, :]
        d_sum = around(d, src[0, near[0], :], src[0, near[1], :])
        m_sum = around(m, src[1, near[0], :], src[1, near[1], :])
        t = [coef[i, rows, :] for i in range(TABLES + 1)]
        dry = 1.0 - m
        m_new = t[1] * m + t[0] * m_sum
        d_new = t[3] * d + t[2] * d_sum + t[4] * (1.0 - d) * (dry * dry)
        return jnp.maximum(d_new, t[5]), m_new

    for src, dst in ((start, ping), (ping, pong), (pong, ping)):
        for g in range(count):
            new = advance(src, g)
            for f in range(2):
                dst[f, pl.ds(ROWS * g, ROWS), :] = new[f]

    for g in range(groups):
        rows = pl.ds(ROWS * g, ROWS)
        new = [v[:, :width] for v in advance(ping, g)]

        pass_on = pltpu.make_async_remote_copy(
            outbox.at[:, rows, :], inbox.at[:, rows, :], chain_send.at[g], chain_recv.at[g],
            device_id={"tm": slot + 1}, device_id_type=pl.DeviceIdType.MESH)

        @pl.when(slot == 0)
        def _():
            for f in range(2):
                outbox[f, rows, :] = new[f]
            pass_on.start()

        @pl.when(slot > 0)
        def _():
            for f in range(2):
                outbox[f, rows, :] = new[f] - factor[f, rows, :] * start[f, rows, pl.ds(0, width)]

    for g in range(groups):
        rows = pl.ds(ROWS * g, ROWS)
        pass_on = pltpu.make_async_remote_copy(
            outbox.at[:, rows, :], inbox.at[:, rows, :], chain_send.at[g], chain_recv.at[g],
            device_id={"tm": slot + 1}, device_id_type=pl.DeviceIdType.MESH)

        @pl.when(slot > 0)
        def _():
            pass_on.wait_recv()
            for f in range(2):
                outbox[f, rows, :] = outbox[f, rows, :] + factor[f, rows, :] * inbox[f, rows, :]

            @pl.when(slot < n_t - 1)
            def _():
                pass_on.start()

        pltpu.make_async_copy(outbox.at[:, rows, :], out_hbm.at[:, rows, :], store_sem.at[g]).start()

    for there, _, copy in sends:
        @pl.when(there)
        def _():
            copy.wait_send()
    for g in range(groups):
        rows = pl.ds(ROWS * g, ROWS)

        @pl.when(slot < n_t - 1)
        def _():
            pltpu.make_async_remote_copy(
                outbox.at[:, rows, :], inbox.at[:, rows, :], chain_send.at[g], chain_recv.at[g],
                device_id={"tm": slot + 1}, device_id_type=pl.DeviceIdType.MESH).wait_send()

        pltpu.make_async_copy(outbox.at[:, rows, :], out_hbm.at[:, rows, :], store_sem.at[g]).wait()


def solution(mesh):
    n_t, n_x, n_y = mesh.shape["tm"], mesh.shape["sx"], mesh.shape["sy"]

    def body(state_old, classes, seeds, material_coef, coarse_decay):
        _, fields, height, width = state_old.shape
        groups = height // ROWS
        f32, dma = jnp.float32, pltpu.SemaphoreType.DMA
        big = (fields, height + ROWS, width + LANES)
        hbm = pl.BlockSpec(memory_space=pl.ANY)
        smem = pl.BlockSpec(memory_space=pltpu.SMEM)
        out = pl.pallas_call(
            functools.partial(kernel, (n_t, n_x, n_y, height, width)),
            out_shape=jax.ShapeDtypeStruct((fields, height, width), f32),
            in_specs=[hbm, hbm, hbm, smem, smem],
            out_specs=hbm,
            scratch_shapes=[
                pltpu.VMEM(big, f32),
                pltpu.VMEM(big, f32),
                pltpu.VMEM(big, f32),
                pltpu.VMEM((TABLES + 1,) + big[1:], f32),
                pltpu.VMEM((fields, height, width), f32),
                pltpu.VMEM((height, width), jnp.int32),
                pltpu.VMEM((height, width), jnp.int32),
                pltpu.VMEM((fields, height, width), f32),
                pltpu.VMEM((fields, height, width), f32),
                pltpu.VMEM((2, 2 * ROWS, width), f32),
                pltpu.VMEM((2, 2 * ROWS, width), f32),
                pltpu.VMEM((2, ROWS, LANES), f32),
                pltpu.VMEM((2, ROWS, LANES), f32),
                pltpu.VMEM((2, 2, ROWS, LANES), f32),
                dma((3,)), dma((2,)), dma((2,)), dma((2,)), dma((2,)),
                dma((2, 2)), dma((2, 2)), dma((groups,)), dma((groups,)), dma((groups,)),
            ],
            compiler_params=pltpu.CompilerParams(
                collective_id=0, has_side_effects=True, vmem_limit_bytes=24 * 1024 * 1024
            ),
        )(state_old[0], classes, seeds, material_coef, coarse_decay)
        return out[None]

    return jax.shard_map(
        body,
        mesh=mesh,
        in_specs=(P("tm", None, "sx", "sy"), P("sx", "sy"), P("sx", "sy"), P(), P()),
        out_specs=P("tm", None, "sx", "sy"),
        check_vma=False,
    )
```

time: 122 us -> 19.8 us (0.16)
  waiting for transfers between devices: 62.7 us -> 0 us
  starting transfers between devices: 34.6 us -> 0 us
  Pallas kernels: 0 us -> 14.8 us
  between operations: 13.8 us -> 0.01 us
  other arithmetic: 8.83 us -> 0 us
  local copies, waits for them, and re-layouts: 0.88 us -> 4.83 us
    all_gather x2 -> x0, waiting for transfers between devices: 43.9 us -> none  [prefix(): gathered = jax.tree.map(lambda a: lax.all_gather(a, axis), part)]
    ppermute x16 -> x0, starting transfers between devices: 34.6 us -> none  [the longest x8 21.6 us: extended(): lax.ppermute(tail, axis, [(i, (i + 1) % count) for i in range(ends)])]
    ppermute x16 -> x0, waiting for transfers between devices: 18.1 us -> none  [the longest x8 11.4 us: extended(): lax.ppermute(head, axis, [((i + 1) % count, i) for i in range(ends)])]
    pallas_call x0 -> x1, Pallas kernels: none -> 14.8 us  [body(): pl.pallas_call(functools.partial(kernel, (n_t, n_x, n_y, height, width)),...]
    unnamed x10 -> x11, local copies, waits for them, and re-layouts: 0.02 us -> 4.83 us
    add x3 -> x0, other arithmetic: 3.56 us -> none  [compose(): return (later[0] * earlier[0], later[0] * earlier[1] + later[1])]
    sub x9 -> x0, other arithmetic: 1.99 us -> none  [the longest x4 0.96 us: advance(): padded[:, 2:, 1:-1] + padded[:, :-2, 1:-1] + padded[:, 1:-1, 2:]]
  transfers between devices with their start and end apart: 18 -> 0, of which waited for: 10 -> 0; matrix products, arithmetic and copies ran while one was open for 1% -> 0% of each run, Pallas kernels for 0% -> 0%
where the time goes in v1:
time: 19.8 us; the launch traced here: 19.6 us
  Pallas kernels  14.8 us (75%)
  local copies, waits for them, and re-layouts  4.83 us (24%)
    pallas_call x1, Pallas kernels, body(): pl.pallas_call(functools.partial(kernel, (n_t, n_x, n_y, height, width)),...  14.8 us
    unnamed x11, local copies, waits for them, and re-layouts  4.83 us

profile of v1, /device:TPU:13, one launch (start us, length us, event | category | flops | bytes accessed | tf_op | source)
XLA Modules:
  0.0 19.6 jit_solution(12014658598123505222)
XLA Ops:
  0.0 0.0 copy-start
  0.0 0.9 %copy-done = f32[1,2,64,512]{3,2,1,0:T(8,128)S(1)} copy-done((f32[1,2,64,512]{3,2,1,0:T(8,128)S(1)}, f32[1,2,64,512]{3,2,1,0:T(8,128)}, u32[]{:S(2)}) %copy-start) | copy-done | bytes 262168
  1.0 0.0 copy-start.1
  1.0 0.9 %copy-done.1 = s32[64,512]{1,0:T(8,128)S(1)} copy-done((s32[64,512]{1,0:T(8,128)S(1)}, s32[64,512]{1,0:T(8,128)}, u32[]{:S(2)}) %copy-start.1) | copy-done | bytes 131096
  1.9 0.0 copy-start.2
  1.9 0.9 %copy-done.2 = s32[64,512]{1,0:T(8,128)S(1)} copy-done((s32[64,512]{1,0:T(8,128)S(1)}, s32[64,512]{1,0:T(8,128)}, u32[]{:S(2)}) %copy-start.2) | copy-done | bytes 131096
  2.8 0.0 copy-start.3
  2.8 0.7 %copy-done.3 = f32[4,2,8]{2,1,0:T(2,128)S(1)} copy-done((f32[4,2,8]{2,1,0:T(2,128)S(1)}, f32[4,2,8]{2,1,0:T(2,128)}, u32[]{:S(2)}) %copy-start.3) | copy-done | bytes 280
  3.4 0.0 copy-start.4
  3.5 0.7 %copy-done.4 = f32[4,8]{1,0:T(4,128)S(1)} copy-done((f32[4,8]{1,0:T(4,128)S(1)}, f32[4,8]{1,0:T(4,128)}, u32[]{:S(2)}) %copy-start.4) | copy-done | bytes 152
  4.1 14.8 %shard_map.55 = f32[2,64,512]{2,1,0:T(8,128)S(1)} custom-call(f32[2,64,512]{2,1,0:T(8,128)S(1)} %bitcast.3, s32[64,512]{1,0:T(8,128)S(1)} %copy-done.1, s32[64,512]{1,0:T(8,128)S(1)} %copy-done.2, f32[4,8]{1,0:T(4,128)S(1)} %copy-done.4, f32[4,2,8]{2,1,0:T(2,128)S(1)} %copy-done.3), custom_call_target="tpu_custom_call" | custom-call | tf_op jit(solution)/shard_map/pallas_call | solution.py:295
  18.9 0.7 %copy.7 = f32[1,2,64,512]{3,2,1,0:T(8,128)} copy(f32[1,2,64,512]{3,2,1,0:T(8,128)S(1)} %bitcast.2) | data formatting | bytes 524288
Async XLA Ops:
  0.0 0.9 %copy-start = (f32[1,2,64,512]{3,2,1,0:T(8,128)S(1)}, f32[1,2,64,512]{3,2,1,0:T(8,128)}, u32[]{:S(2)}) copy-start(f32[1,2,64,512]{3,2,1,0:T(8,128)} %param.5) | copy-start | bytes 786436
  1.0 0.9 %copy-start.1 = (s32[64,512]{1,0:T(8,128)S(1)}, s32[64,512]{1,0:T(8,128)}, u32[]{:S(2)}) copy-start(s32[64,512]{1,0:T(8,128)} %classes_hbm.1) | copy-start | bytes 393220
  1.9 0.9 %copy-start.2 = (s32[64,512]{1,0:T(8,128)S(1)}, s32[64,512]{1,0:T(8,128)}, u32[]{:S(2)}) copy-start(s32[64,512]{1,0:T(8,128)} %seeds_hbm.1) | copy-start | bytes 393220
  2.8 0.7 %copy-start.3 = (f32[4,2,8]{2,1,0:T(2,128)S(1)}, f32[4,2,8]{2,1,0:T(2,128)}, u32[]{:S(2)}) copy-start(f32[4,2,8]{2,1,0:T(2,128)} %decay.1) | copy-start | bytes 772
  3.4 0.7 %copy-start.4 = (f32[4,8]{1,0:T(4,128)S(1)}, f32[4,8]{1,0:T(4,128)}, u32[]{:S(2)}) copy-start(f32[4,8]{1,0:T(4,128)} %mat.1) | copy-start | bytes 388

commit v2 on v1

--- a/solution.py
+++ b/solution.py
@@ -24,8 +24,8 @@
 
 
 def kernel(
-    sizes, state_hbm, classes_hbm, seeds_hbm, mat, decay, out_hbm,
-    start, ping, pong, coef, factor, cls, sds, inbox, outbox,
+    sizes, state_hbm, classes_hbm, seeds_hbm, mat_hbm, decay_hbm, out_hbm,
+    mat, decay, start, ping, pong, coef, factor, cls, sds, inbox, outbox,
     row_out, row_in, col_out, col_in, diag_in,
     load_sem, row_send, row_recv, col_send, col_recv, diag_send, diag_recv, chain_send, chain_recv, store_sem,
 ):
@@ -51,6 +51,8 @@
         pltpu.make_async_copy(state_hbm, start.at[:, pl.ds(0, height), pl.ds(0, width)], load_sem.at[0]),
         pltpu.make_async_copy(classes_hbm, cls, load_sem.at[1]),
         pltpu.make_async_copy(seeds_hbm, sds, load_sem.at[2]),
+        pltpu.make_async_copy(mat_hbm, mat, load_sem.at[3]),
+        pltpu.make_async_copy(decay_hbm, decay, load_sem.at[4]),
     ]
     for load in loads:
         load.start()
@@ -290,14 +292,15 @@
         groups = height // ROWS
         f32, dma = jnp.float32, pltpu.SemaphoreType.DMA
         big = (fields, height + ROWS, width + LANES)
-        hbm = pl.BlockSpec(memory_space=pl.ANY)
-        smem = pl.BlockSpec(memory_space=pltpu.SMEM)
+        hbm = pl.BlockSpec(memory_space=pltpu.HBM)
         out = pl.pallas_call(
             functools.partial(kernel, (n_t, n_x, n_y, height, width)),
             out_shape=jax.ShapeDtypeStruct((fields, height, width), f32),
-            in_specs=[hbm, hbm, hbm, smem, smem],
+            in_specs=[hbm] * 5,
             out_specs=hbm,
             scratch_shapes=[
+                pltpu.SMEM(material_coef.shape, f32),
+                pltpu.SMEM(coarse_decay.shape, f32),
                 pltpu.VMEM(big, f32),
                 pltpu.VMEM(big, f32),
                 pltpu.VMEM(big, f32),
@@ -312,11 +315,11 @@
                 pltpu.VMEM((2, ROWS, LANES), f32),
                 pltpu.VMEM((2, ROWS, LANES), f32),
                 pltpu.VMEM((2, 2, ROWS, LANES), f32),
-                dma((3,)), dma((2,)), dma((2,)), dma((2,)), dma((2,)),
+                dma((5,)), dma((2,)), dma((2,)), dma((2,)), dma((2,)),
                 dma((2, 2)), dma((2, 2)), dma((groups,)), dma((groups,)), dma((groups,)),
             ],
             compiler_params=pltpu.CompilerParams(
-                collective_id=0, has_side_effects=True, vmem_limit_bytes=24 * 1024 * 1024
+                collective_id=0, has_side_effects=True, vmem_limit_bytes=61 * 1024 * 1024
             ),
         )(state_old[0], classes, seeds, material_coef, coarse_decay)
         return out[None]

time: 19.8 us -> 16.2 us (0.82)
  local copies, waits for them, and re-layouts: 4.83 us -> 1.67 us
  Pallas kernels: 14.8 us -> 14.3 us
    unnamed x11 -> x1, local copies, waits for them, and re-layouts: 4.83 us -> 1.67 us
    pallas_call x1, Pallas kernels: 14.8 us -> 14.3 us  [body(): pl.pallas_call(functools.partial(kernel, (n_t, n_x, n_y, height, width)),...]
where the time goes in v2:
time: 16.2 us; the launch traced here: 16 us
  Pallas kernels  14.3 us (88%)
  local copies, waits for them, and re-layouts  1.67 us (10%)
    pallas_call x1, Pallas kernels, body(): pl.pallas_call(functools.partial(kernel, (n_t, n_x, n_y, height, width)),...  14.3 us
    unnamed x1, local copies, waits for them, and re-layouts  1.67 us

profile of v2, /device:TPU:13, one launch (start us, length us, event | category | flops | bytes accessed | tf_op | source)
XLA Modules:
  0.0 16.0 jit_solution(16918103684119193061)
XLA Ops:
  0.0 14.3 %shard_map.55 = f32[2,64,512]{2,1,0:T(8,128)} custom-call(f32[2,64,512]{2,1,0:T(8,128)} %bitcast.3, s32[64,512]{1,0:T(8,128)} %classes_hbm.1, s32[64,512]{1,0:T(8,128)} %seeds_hbm.1, f32[4,8]{1,0:T(4,128)} %mat_hbm.1, f32[4,2,8]{2,1,0:T(2,128)} %decay_hbm.1), custom_call_target="tpu_custom_call" | custom-call | tf_op jit(solution)/shard_map/pallas_call | solution.py:296
  14.3 1.7 %copy.7 = f32[1,2,64,512]{3,2,1,0:T(8,128)} copy(f32[1,2,64,512]{3,2,1,0:T(8,128)} %bitcast.2) | data formatting | bytes 524288

commit v3 on v2

--- a/solution.py
+++ b/solution.py
@@ -24,10 +24,10 @@
 
 
 def kernel(
-    sizes, state_hbm, classes_hbm, seeds_hbm, mat_hbm, decay_hbm, out_hbm,
-    mat, decay, start, ping, pong, coef, factor, cls, sds, inbox, outbox,
+    sizes, state_hbm, classes_hbm, seeds_hbm, mat_hbm, decay_hbm, outbox,
+    mat, decay, start, ping, pong, coef, factor, cls, sds, inbox,
     row_out, row_in, col_out, col_in, diag_in,
-    load_sem, row_send, row_recv, col_send, col_recv, diag_send, diag_recv, chain_send, chain_recv, store_sem,
+    load_sem, row_send, row_recv, col_send, col_recv, diag_send, diag_recv, chain_send, chain_recv,
 ):
     n_t, n_x, n_y, height, width = sizes
     groups = height // ROWS
@@ -266,8 +266,6 @@
             def _():
                 pass_on.start()
 
-        pltpu.make_async_copy(outbox.at[:, rows, :], out_hbm.at[:, rows, :], store_sem.at[g]).start()
-
     for there, _, copy in sends:
         @pl.when(there)
         def _():
@@ -280,8 +278,6 @@
             pltpu.make_async_remote_copy(
                 outbox.at[:, rows, :], inbox.at[:, rows, :], chain_send.at[g], chain_recv.at[g],
                 device_id={"tm": slot + 1}, device_id_type=pl.DeviceIdType.MESH).wait_send()
-
-        pltpu.make_async_copy(outbox.at[:, rows, :], out_hbm.at[:, rows, :], store_sem.at[g]).wait()
 
 
 def solution(mesh):
@@ -295,9 +291,9 @@
         hbm = pl.BlockSpec(memory_space=pltpu.HBM)
         out = pl.pallas_call(
             functools.partial(kernel, (n_t, n_x, n_y, height, width)),
-            out_shape=jax.ShapeDtypeStruct((fields, height, width), f32),
+            out_shape=pltpu.VMEM((fields, height, width), f32),
             in_specs=[hbm] * 5,
-            out_specs=hbm,
+            out_specs=pl.BlockSpec(memory_space=pltpu.VMEM),
             scratch_shapes=[
                 pltpu.SMEM(material_coef.shape, f32),
                 pltpu.SMEM(coarse_decay.shape, f32),
@@ -309,17 +305,16 @@
                 pltpu.VMEM((height, width), jnp.int32),
                 pltpu.VMEM((height, width), jnp.int32),
                 pltpu.VMEM((fields, height, width), f32),
-                pltpu.VMEM((fields, height, width), f32),
                 pltpu.VMEM((2, 2 * ROWS, width), f32),
                 pltpu.VMEM((2, 2 * ROWS, width), f32),
                 pltpu.VMEM((2, ROWS, LANES), f32),
                 pltpu.VMEM((2, ROWS, LANES), f32),
                 pltpu.VMEM((2, 2, ROWS, LANES), f32),
                 dma((5,)), dma((2,)), dma((2,)), dma((2,)), dma((2,)),
-                dma((2, 2)), dma((2, 2)), dma((groups,)), dma((groups,)), dma((groups,)),
+                dma((2, 2)), dma((2, 2)), dma((groups,)), dma((groups,)),
             ],
             compiler_params=pltpu.CompilerParams(
-                collective_id=0, has_side_effects=True, vmem_limit_bytes=61 * 1024 * 1024
+                collective_id=0, has_side_effects=True, vmem_limit_bytes=60 * 1024 * 1024
             ),
         )(state_old[0], classes, seeds, material_coef, coarse_decay)
         return out[None]

time: 16.2 us -> 14.5 us (0.90)
  local copies, waits for them, and re-layouts: 1.67 us -> 0.71 us
  Pallas kernels: 14.3 us -> 13.7 us
    unnamed x1, local copies, waits for them, and re-layouts: 1.67 us -> 0.71 us
    pallas_call x1, Pallas kernels: 14.3 us -> 13.7 us  [body(): pl.pallas_call(functools.partial(kernel, (n_t, n_x, n_y, height, width)),...]
where the time goes in v3:
time: 14.5 us; the launch traced here: 14.4 us
  Pallas kernels  13.7 us (94%)
  local copies, waits for them, and re-layouts  0.71 us (5%)
    pallas_call x1, Pallas kernels, body(): pl.pallas_call(functools.partial(kernel, (n_t, n_x, n_y, height, width)),...  13.7 us
    unnamed x1, local copies, waits for them, and re-layouts  0.71 us

profile of v3, /device:TPU:13, one launch (start us, length us, event | category | flops | bytes accessed | tf_op | source)
XLA Modules:
  0.0 14.4 jit_solution(17897327366235481809)
XLA Ops:
  0.0 13.7 %shard_map.55 = f32[2,64,512]{2,1,0:T(8,128)S(1)} custom-call(f32[2,64,512]{2,1,0:T(8,128)} %bitcast.3, s32[64,512]{1,0:T(8,128)} %classes_hbm.1, s32[64,512]{1,0:T(8,128)} %seeds_hbm.1, f32[4,8]{1,0:T(4,128)} %mat_hbm.1, f32[4,2,8]{2,1,0:T(2,128)} %decay_hbm.1), custom_call_target="tpu_custom_call" | custom-call | tf_op jit(solution)/shard_map/pallas_call | solution.py:292
  13.7 0.7 %copy.7 = f32[1,2,64,512]{3,2,1,0:T(8,128)} copy(f32[1,2,64,512]{3,2,1,0:T(8,128)S(1)} %bitcast.2) | data formatting | bytes 524288
